TPU v7x, 256 devices: a whole 4x4x8 slice. The times are simulated.
256 devices in a mesh: row: 64 (over z, x, core), col: 4 (over y).
Axes of the slice: x: 4, y: 4, z: 8, core: 2. Of those that a mesh axis runs over, the one named last changes fastest.
Arguments:
- y_prev: float32 [32768, 128], P(('row', 'col'))
- step_prev: float32 [32768, 128], P(('row', 'col')), may hold values from -3 to 3
- accept: int32 [256], P(('row', 'col')), may hold values 0 or 1
- blocks: bfloat16 [64, 4, 192, 128, 128], P('row', 'col'), as said below
- blk_row: int32 [64, 4, 192], P('row', 'col'), may hold values from 0 to 3
- blk_col: int32 [64, 4, 192], P('row', 'col'), may hold values from 0 to 63
Outputs:
- step: float32 [32768, 128], P(('row', 'col'))
- residual: float32 [32768, 128], P(('row', 'col'))
Inputs may be any that keep to these rules, and one draw needn't show every extreme that they name: `blocks`: edge weights.
All inputs are finite; a program needn't handle non-finite values. No bound on the sum of `accept` on one device may be relied on, other than what follows from the above.
Results may differ from a plain program's by a relative error of at most 0.035.
Values may be sent and summed in bfloat16 or wider, within the bound.
A program may use at most 64 MiB of HBM per device.

v0:
```python
import jax
import jax.numpy as jnp
from jax import lax
from jax.sharding import PartitionSpec as P

ITERS = 3


damping = 14.0


def normalize(rows):
    return rows * lax.rsqrt(jnp.sum(rows * rows, axis=1, keepdims=True) + 1e-06)


def shards(y_prev, step_prev, accept, blocks, blk_row, blk_col):
    tiles_own = blocks[0, 0]
    rows_index = blk_row[0, 0]
    cols_index = blk_col[0, 0]
    n_col = lax.axis_size("col")
    own_rows = y_prev.shape[0]
    width = y_prev.shape[1]
    side = tiles_own.shape[1]
    group_blocks = own_rows * n_col // side
    onehot = (rows_index[None, :] == jnp.arange(group_blocks, dtype=jnp.int32)[:, None]).astype(
        jnp.float32
    )

    def apply_graph(vector):
        gathered = lax.all_gather(vector.astype(jnp.bfloat16), "row", axis=0, tiled=True)
        tiles = gathered.reshape(-1, side, width)
        prods = jnp.einsum(
            "sab,sbd->sad", tiles_own, tiles[cols_index], preferred_element_type=jnp.float32
        )
        partial_rows = jnp.einsum("rs,sad->rad", onehot, prods).reshape(group_blocks * side, width)
        return 2.0 * lax.psum_scatter(partial_rows, "col", scatter_dimension=0, tiled=True)

    taken = accept.astype(jnp.float32)[:, None, None]
    moved = y_prev.reshape(-1, side, width) + taken * step_prev.reshape(-1, side, width)
    point = normalize(moved.reshape(own_rows, width))
    full_grad = apply_graph(point)
    lam = jnp.sum(point * full_grad, axis=1, keepdims=True)
    grad = full_grad - lam * point
    residual = -grad
    direction = residual
    step = jnp.zeros_like(residual)
    norm_now = lax.psum(jnp.sum(residual * residual), ("row", "col"))
    for turn in range(ITERS):
        image = apply_graph(direction)
        image = image - jnp.sum(point * image, axis=1, keepdims=True) * point
        image = image - lam * direction + damping * direction
        curv = lax.psum(jnp.sum(direction * image), ("row", "col"))
        alpha = norm_now / curv
        step = step + alpha * direction
        residual = residual - alpha * image
        norm_next = lax.psum(jnp.sum(residual * residual), ("row", "col"))
        direction = residual + norm_next / norm_now * direction
        norm_now = norm_next
    return (step, residual)


def solution(mesh):
    placed = (
        P(("row", "col"), None),
        P(("row", "col"), None),
        P(("row", "col")),
        P("row", "col", None, None, None),
        P("row", "col", None),
        P("row", "col", None),
    )
    return jax.shard_map(
        shards,
        mesh=mesh,
        in_specs=placed,
        out_specs=(P(("row", "col"), None), P(("row", "col"), None)),
        check_vma=False,
    )
```

profile of v0, /device:TPU:1, one launch (start us, length us, event | category | flops | bytes accessed | tf_op | source)
XLA Modules:
  0.0 944.9 jit_solution(17028964993869593908)
XLA Ops:
  7.9 1.0 multiply_reduce_fusion.10
  8.8 0.7 multiply_convert_fusion
  9.6 0.7 compare_select_fusion
  10.3 82.5 %all-gather.5.cloned.1.call-done = bf16[8192,128]{1,0:T(8,128)(2,1)} async-done(((bf16[128,128]{1,0:T(8,128)(2,1)}), bf16[8192,128]{1,0:T(8,128)(2,1)}) %all-gather.5.cloned.1.call-update) | async-done | bytes 2097168 | tf_op jit(solution)/shard_map/all_gather | solution.py:30
  92.8 9.6 %gather_fusion = bf16[192,128,128]{2,1,0:T(8,128)(2,1)} fusion(bf16[64,128,128]{2,1,0:T(8,128)(2,1)} %bitcast.44, s32[1024]{0:T(1024)S(1)} %pad_clamp_fusion), kind=kCustom, calls=%fused_computation | custom fusion | bytes 12583680 | tf_op jit(solution)/shard_map/gather | solution.py:33
  102.4 11.8 %fusion.14 = bf16[192,128,128]{2,1,0:T(8,128)(2,1)} fusion(bf16[192,128,128]{2,1,0:T(8,128)(2,1)} %gather_fusion, bf16[1,1,192,128,128]{4,3,2,1,0:T(8,128)(2,1)} %param.9), kind=kOutput, calls=%fused_computation.18 | convolution fusion | flops 805306368 | bytes 18874368 | tf_op jit(solution)/shard_map/sab,sbd->sad/dot_general | solution.py:32
  114.2 9.0 copy.12
  123.2 3.7 fusion.6
  126.9 0.7 copy.8
  127.7 18.4 %reduce-scatter.5.cloned.1.call-done = f32[128,128]{1,0:T(8,128)} async-done(((f32[512,128]{1,0:T(8,128)}), f32[128,128]{1,0:T(8,128)}) %reduce-scatter.5.cloned.1.call-update) | async-done | bytes 65552 | tf_op jit(solution)/shard_map/reduce_scatter | solution.py:36
  146.1 1.0 multiply_reduce_fusion.9
  147.1 1.6 negate_convert_fusion
  148.9 80.5 %all-gather.7.cloned.1.call-done = bf16[8192,128]{1,0:T(8,128)(2,1)} async-done(((bf16[128,128]{1,0:T(8,128)(2,1)}), bf16[8192,128]{1,0:T(8,128)(2,1)}) %all-gather.7.cloned.1.call-update) | async-done | bytes 2097168 | tf_op jit(solution)/shard_map/all_gather | solution.py:30
  229.4 9.6 %gather_fusion.1 = bf16[192,128,128]{2,1,0:T(8,128)(2,1)} fusion(bf16[64,128,128]{2,1,0:T(8,128)(2,1)} %bitcast.46, s32[1024]{0:T(1024)S(1)} %pad_clamp_fusion), kind=kCustom, calls=%fused_computation.1 | custom fusion | bytes 12583680 | tf_op jit(solution)/shard_map/gather | solution.py:33
  239.0 11.8 %fusion.12 = bf16[192,128,128]{2,1,0:T(8,128)(2,1)} fusion(bf16[192,128,128]{2,1,0:T(8,128)(2,1)} %gather_fusion.1, bf16[1,1,192,128,128]{4,3,2,1,0:T(8,128)(2,1)} %param.9), kind=kOutput, calls=%fused_computation.16 | convolution fusion | flops 805306368 | bytes 18874368 | tf_op jit(solution)/shard_map/sab,sbd->sad/dot_general | solution.py:32
  250.8 9.0 copy.13
  259.8 3.7 fusion.4
  263.5 0.7 copy.9
  264.3 18.4 %reduce-scatter.7.cloned.1.call-done = f32[128,128]{1,0:T(8,128)} async-done(((f32[512,128]{1,0:T(8,128)}), f32[128,128]{1,0:T(8,128)}) %reduce-scatter.7.cloned.1.call-update) | async-done | bytes 65552 | tf_op jit(solution)/shard_map/reduce_scatter | solution.py:36
  282.7 1.0 multiply_reduce_fusion.7
  283.7 1.6 multiply_reduce_fusion.6
  285.3 78.2 %all-reduce = (f32[]{:T(128)}, f32[]{:T(128)}) all-reduce(f32[]{:T(128)} %get-tuple-element.3, f32[]{:T(128)} %get-tuple-element.2), channel_id=1, replica_groups=mesh['row'=64,'col'=4] {'row','col'}, use_global_device_ids=true, to_apply=%region_4.0 | all-reduce | flops 2 | bytes 16 | tf_op jit(solution)/shard_map/psum | solution.py:47
  364.8 1.6 multiply_reduce_fusion.5
  366.4 73.3 %psum.44 = f32[]{:T(128)} all-reduce(f32[]{:T(128)} %get-tuple-element.10), channel_id=1, replica_groups=mesh['row'=64,'col'=4] {'row','col'}, use_global_device_ids=true, to_apply=%region_10.0 | all-reduce | flops 1 | bytes 8 | tf_op jit(solution)/shard_map/psum | solution.py:56
  440.9 0.6 fusion.22
  441.9 73.5 %all-gather.9.cloned.1.call-done = bf16[8192,128]{1,0:T(8,128)(2,1)} async-done(((bf16[128,128]{1,0:T(8,128)(2,1)}), bf16[8192,128]{1,0:T(8,128)(2,1)}) %all-gather.9.cloned.1.call-update) | async-done | bytes 2097168 | tf_op jit(solution)/shard_map/all_gather | solution.py:30
  515.3 9.6 %gather_fusion.2 = bf16[192,128,128]{2,1,0:T(8,128)(2,1)} fusion(bf16[64,128,128]{2,1,0:T(8,128)(2,1)} %bitcast.47, s32[1024]{0:T(1024)S(1)} %pad_clamp_fusion), kind=kCustom, calls=%fused_computation.2 | custom fusion | bytes 12583680 | tf_op jit(solution)/shard_map/gather | solution.py:33
  525.0 11.8 %fusion.10 = bf16[192,128,128]{2,1,0:T(8,128)(2,1)} fusion(bf16[192,128,128]{2,1,0:T(8,128)(2,1)} %gather_fusion.2, bf16[1,1,192,128,128]{4,3,2,1,0:T(8,128)(2,1)} %param.9), kind=kOutput, calls=%fused_computation.14 | convolution fusion | flops 805306368 | bytes 18874368 | tf_op jit(solution)/shard_map/sab,sbd->sad/dot_general | solution.py:32
  536.8 9.0 copy.14
  545.8 3.7 fusion.2
  549.5 0.7 copy.10
  550.2 18.4 %reduce-scatter.9.cloned.1.call-done = f32[128,128]{1,0:T(8,128)} async-done(((f32[512,128]{1,0:T(8,128)}), f32[128,128]{1,0:T(8,128)}) %reduce-scatter.9.cloned.1.call-update) | async-done | bytes 65552 | tf_op jit(solution)/shard_map/reduce_scatter | solution.py:36
  568.6 1.0 multiply_reduce_fusion.4
  569.6 1.6 multiply_reduce_fusion.3
  571.2 78.1 %psum.45 = f32[]{:T(128)} all-reduce(f32[]{:T(128)} %multiply_reduce_fusion.3), channel_id=1, replica_groups=mesh['row'=64,'col'=4] {'row','col'}, use_global_device_ids=true, to_apply=%region_14.0 | all-reduce | flops 1 | bytes 8 | tf_op jit(solution)/shard_map/psum | solution.py:52
  650.6 1.6 multiply_reduce_fusion.2
  652.1 73.3 %psum.46 = f32[]{:T(128)} all-reduce(f32[]{:T(128)} %get-tuple-element.6), channel_id=1, replica_groups=mesh['row'=64,'col'=4] {'row','col'}, use_global_device_ids=true, to_apply=%region_16.0 | all-reduce | flops 1 | bytes 8 | tf_op jit(solution)/shard_map/psum | solution.py:56
  727.7 73.5 %all-gather.11.cloned.1.call-done = bf16[8192,128]{1,0:T(8,128)(2,1)} async-done(((bf16[128,128]{1,0:T(8,128)(2,1)}), bf16[8192,128]{1,0:T(8,128)(2,1)}) %all-gather.11.cloned.1.call-update) | async-done | bytes 2097168 | tf_op jit(solution)/shard_map/all_gather | solution.py:30
  801.2 9.6 %gather_fusion.3 = bf16[192,128,128]{2,1,0:T(8,128)(2,1)} fusion(bf16[64,128,128]{2,1,0:T(8,128)(2,1)} %bitcast.45, s32[1024]{0:T(1024)S(1)} %pad_clamp_fusion), kind=kCustom, calls=%fused_computation.3 | custom fusion | bytes 12583680 | tf_op jit(solution)/shard_map/gather | solution.py:33
  810.8 11.8 %fusion.8 = bf16[192,128,128]{2,1,0:T(8,128)(2,1)} fusion(bf16[192,128,128]{2,1,0:T(8,128)(2,1)} %gather_fusion.3, bf16[1,1,192,128,128]{4,3,2,1,0:T(8,128)(2,1)} %param.9), kind=kOutput, calls=%fused_computation.12 | convolution fusion | flops 805306368 | bytes 18874368 | tf_op jit(solution)/shard_map/sab,sbd->sad/dot_general | solution.py:32
  822.6 9.0 copy.15
  831.6 3.7 fusion
  835.3 0.7 copy.11
  836.1 18.4 %reduce-scatter.11.cloned.1.call-done = f32[128,128]{1,0:T(8,128)} async-done(((f32[512,128]{1,0:T(8,128)}), f32[128,128]{1,0:T(8,128)}) %reduce-scatter.11.cloned.1.call-update) | async-done | bytes 65552 | tf_op jit(solution)/shard_map/reduce_scatter | solution.py:36
  854.5 1.0 multiply_reduce_fusion.1
  855.5 1.6 multiply_reduce_fusion
  857.1 78.1 %psum.47 = f32[]{:T(128)} all-reduce(f32[]{:T(128)} %multiply_reduce_fusion), channel_id=1, replica_groups=mesh['row'=64,'col'=4] {'row','col'}, use_global_device_ids=true, to_apply=%region_20.0 | all-reduce | flops 1 | bytes 8 | tf_op jit(solution)/shard_map/psum | solution.py:52
  936.5 1.6 multiply_subtract_fusion
  (21 shorter events, 1.8 us)
Async XLA Ops:
  7.2 85.6 %all-gather.5.cloned.1.call-start = ((), (), s32[]{:S(2)}) async-start(), calls=%async_computation.4 | async-start | bytes 2129920 | tf_op jit(solution)/shard_map/all_gather | solution.py:30
  9.6 136.5 %reduce-scatter.5.cloned.1.call-start = ((), (), s32[]{:S(2)}) async-start(), calls=%async_computation.5 | async-start | bytes 327680 | tf_op jit(solution)/shard_map/reduce_scatter | solution.py:36
  114.2 9.0 copy-start
  127.7 101.7 %all-gather.7.cloned.1.call-start = ((), (), s32[]{:S(2)}) async-start(), calls=%async_computation.6 | async-start | bytes 2129920 | tf_op jit(solution)/shard_map/all_gather | solution.py:30
  148.7 134.0 %reduce-scatter.7.cloned.1.call-start = ((), (), s32[]{:S(2)}) async-start(), calls=%async_computation.7 | async-start | bytes 327680 | tf_op jit(solution)/shard_map/reduce_scatter | solution.py:36
  264.3 251.1 %all-gather.9.cloned.1.call-start = ((), (), s32[]{:S(2)}) async-start(), calls=%async_computation.8 | async-start | bytes 2129920 | tf_op jit(solution)/shard_map/all_gather | solution.py:30
  441.6 127.0 %reduce-scatter.9.cloned.1.call-start = ((), (), s32[]{:S(2)}) async-start(), calls=%async_computation.9 | async-start | bytes 327680 | tf_op jit(solution)/shard_map/reduce_scatter | solution.py:36
  550.2 251.0 %all-gather.11.cloned.1.call-start = ((), (), s32[]{:S(2)}) async-start(), calls=%async_computation.10 | async-start | bytes 2129920 | tf_op jit(solution)/shard_map/all_gather | solution.py:30
  727.4 127.1 %reduce-scatter.11.cloned.1.call-start = ((), (), s32[]{:S(2)}) async-start(), calls=%async_computation.11 | async-start | bytes 327680 | tf_op jit(solution)/shard_map/reduce_scatter | solution.py:36
Sparse Core Ops, SparseCore 0:
  11.3 81.3 all-gather.4
  127.8 18.2 reduce-scatter.4
  149.8 79.5 all-gather.6
  264.4 18.2 reduce-scatter.6
  441.7 73.5 all-gather.8
  550.3 18.2 reduce-scatter.8
  727.5 73.6 all-gather.10
  836.2 18.2 reduce-scatter.10
where the time goes:
time: 947 us; the launch traced here: 945 us
  waiting for transfers between devices  384 us (41%)
  blocking collectives  381 us (40%)
  local copies, waits for them, and re-layouts  77.4 us (8%)
  matrix products  62 us (7%)
  between operations  21.4 us (2%)
  other arithmetic  18.7 us (2%)
    all_gather x4, waiting for transfers between devices, apply_graph(): lax.all_gather(vector.astype(jnp.bfloat16), 'row', axis=0, tiled=True)  310 us
    psum x2, blocking collectives, shards(): curv = lax.psum(jnp.sum(direction * image), ('row', 'col'))  156 us
    psum x2, blocking collectives, shards(): norm_next = lax.psum(jnp.sum(residual * residual), ('row', 'col'))  147 us
    psum x1, blocking collectives, shards(): norm_now = lax.psum(jnp.sum(residual * residual), ('row', 'col'))  78.2 us
    reduce_scatter x4, waiting for transfers between devices, apply_graph(): lax.psum_scatter(partial_rows, 'col', scatter_dimension=0, tiled=True)  73.5 us
    dot_general x4, matrix products, apply_graph(): jnp.einsum('sab,sbd->sad', tiles_own, tiles[cols_index], preferred_elemen...  47.2 us
    gather x4, local copies, waits for them, and re-layouts, apply_graph(): tiles[cols_index]  38.6 us
    dot_general x4, local copies, waits for them, and re-layouts, apply_graph(): jnp.einsum('sab,sbd->sad', tiles_own, tiles[cols_index], preferred_elemen...  36 us
  transfers between devices with their start and end apart: 8, of which 8 were waited for; matrix products, arithmetic and copies ran while one was open for 0% of the time, Pallas kernels for 0%

commit v1 on v0

v1 whole, which is shorter than its diff:
```python
import functools

import jax
import jax.numpy as jnp
from jax import lax
from jax.experimental import pallas as pl
from jax.experimental.pallas import tpu as pltpu
from jax.sharding import PartitionSpec as P

MESH = pl.DeviceIdType.MESH
ITERS = 3
DAMPING = 14.0
NZ, NX, NY = 8, 4, 4
SIDE = 128
GROUP = 4
TILES = 64
Z_ORDER = (1, 7, 2, 6, 3, 5, 4)
X_ORDER = (2, 1, 3)
D_ORDER = (0,) + Z_ORDER
PAIRS = ((0, 0), (0, 1), (0, 2), (1, 1), (1, 2), (2, 2), (0, 3), (1, 3), (2, 3))
F32 = jnp.float32
BF16 = jnp.bfloat16
I32 = jnp.int32


def device(z, x, core, y):
    return ((z % NZ * NX + x % NX) * 2 + core % 2, y % NY)


def row_sum(a):
    return jnp.sum(a, axis=1, keepdims=True)


def slot_plan(rows, cols, z, x, core):
    slots = rows.shape[1]
    far = jnp.concatenate([rows, jnp.zeros((1, 256 - slots), I32)], axis=1)
    col = jnp.concatenate([cols, jnp.zeros((1, 256 - slots), I32)], axis=1)
    lane = lax.broadcasted_iota(I32, (1, 256), 1)
    dz = (z + NZ - col // 8) % NZ
    dx = (x + NX - (col // 2) % NX) % NX
    rel = (col + core) % 2
    key_row = jnp.where(lane < slots, ((rel * NZ + dz) * NX + dx) * GROUP + far, 1 << 12)
    sub2 = lax.broadcasted_iota(I32, (256, 256), 0)
    lane2 = lax.broadcasted_iota(I32, (256, 256), 1)
    key_r = jnp.broadcast_to(key_row, (256, 256))
    key_col = jnp.sum(jnp.where(sub2 == lane2, key_r, 0), axis=1, keepdims=True)
    key_c = jnp.broadcast_to(key_col, (256, 256))
    same_before = jnp.sum(jnp.where((key_r == key_c) & (lane2 < sub2), 1, 0), axis=1, keepdims=True)
    place = same_before + jnp.sum(jnp.where(key_r < key_c, 1, 0), axis=1, keepdims=True)
    here = jnp.broadcast_to(place, (256, 256)) == lane2
    order = jnp.sum(jnp.where(here, sub2, 0), axis=0, keepdims=True)
    keep = jnp.sum(jnp.where(here & (jnp.broadcast_to(same_before, (256, 256)) > 0), 1, 0), axis=0, keepdims=True)
    upto = jnp.sum(jnp.where(key_c <= lane2, 1, 0), axis=0, keepdims=True)
    found = jnp.sum(jnp.where(key_c == lane2, 1, 0), axis=0, keepdims=True)
    last = jnp.where(found > 0, upto - 1, slots)
    return jnp.concatenate([order, keep, last, jnp.zeros((5, 256), I32)], axis=0)


def kernel(
    slots, y_ref, step_ref, accept_ref, row_ref, col_ref, blocks_ref, out_step, out_res,
    raw, comp, dense, gat, acc, point, lam, vs, part, got, ar_own, ar_buf, theta, plan_v, plan_s,
    local_sem, gs, zr, xr, cr, ps, pr, ars, arr,
):
    row = lax.axis_index("row")
    y = lax.axis_index("col")
    z, x, core = row // (2 * NX), row // 2 % NX, row % 2

    first = [(dz, dk) for dz in range(NZ) for dk in range(2)]
    second = [(dx, dy) for dx in range(NX) for dy in range(NY)]
    peers = [[device(z + dz, x, core + dk, y) for dz, dk in first], [device(z, x + dx, core, y + dy) for dx, dy in second]]

    barrier = pltpu.get_barrier_semaphore()
    for stage in range(2):
        for peer in peers[stage][1:]:
            pl.semaphore_signal(barrier, inc=1, device_id=peer, device_id_type=MESH)
    blocks_copy = pltpu.make_async_copy(blocks_ref, raw, local_sem.at[0])
    blocks_copy.start()

    moved = y_ref[...] + accept_ref[0].astype(F32) * step_ref[...]
    unit = moved * lax.rsqrt(row_sum(moved * moved) + 1e-06)
    point[...] = unit
    gat[0, 0] = unit.astype(BF16)
    vs[0] = jnp.zeros((SIDE, SIDE), F32)
    lam[...] = jnp.zeros((SIDE, SIDE), F32)
    theta[...] = jnp.zeros((8, SIDE), F32)
    plan_v[...] = slot_plan(row_ref[...], col_ref[...], z, x, core)
    plan_copy = pltpu.make_async_copy(plan_v, plan_s, local_sem.at[1])
    plan_copy.start()
    comp[slots] = jnp.zeros((SIDE, SIDE), BF16)
    pl.semaphore_wait(barrier, len(first) + len(second) - 2)

    def remote(src, dst, send, recv, peer):
        return pltpu.make_async_remote_copy(
            src_ref=src, dst_ref=dst, send_sem=send, recv_sem=recv, device_id=peer, device_id_type=MESH
        )

    def reduce_send(use, stage):
        for j in range(1, 16):
            remote(
                ar_own.at[use, stage], ar_buf.at[use, stage, j], ars.at[use, stage], arr.at[use, stage], peers[stage][j]
            ).start()

    def reduce_take(use, stage):
        for sem in (arr, ars):
            whole = ar_buf.at[use, stage, pl.ds(1, 15)]
            pltpu.make_async_copy(whole, whole, sem.at[use, stage]).wait()
        return ar_own[use, stage] + jnp.sum(ar_buf[use, stage, 1:16], axis=0)

    def compact(start, count):
        def one(j, total):
            keep = plan_s[1, j].astype(F32)
            total = keep * total + raw[plan_s[0, j]].astype(F32)
            comp[j] = total.astype(BF16)
            return total

        return functools.partial(lax.fori_loop, start, start + count, one)

    def densify(chunk):
        def one(q, carry):
            dx, r = q // GROUP, q % GROUP
            dense[chunk, pl.ds(r * SIDE, SIDE), :] = jnp.concatenate(
                [comp[plan_s[2, chunk * 16 + i * GROUP + r]] for i in range(NX)], axis=1
            )
            return carry

        def rows(r, carry):
            return one(r, carry)

        lax.fori_loop(0, GROUP, rows, 0)

    def product(k, carry):
        p = k % 2

        def tile(d, dx):
            return gat.at[p, d * NX + dx]

        def z_copy(d):
            return remote(tile(0, 0), tile(d, 0), gs.at[p], zr.at[p, d], device(z + d, x, core, y))

        def x_copy(d, dx):
            return remote(tile(d, 0), tile(d, dx), gs.at[p], xr.at[p, d, dx], device(z, x + dx, core, y))

        def relay(d):
            return remote(
                gat.at[p, pl.ds(d * NX, NX)], gat.at[p, pl.ds(32 + d * NX, NX)], gs.at[p], cr.at[p, d],
                device(z, x, core + 1, y),
            )

        for d in Z_ORDER:
            z_copy(d).start()
        for dx in X_ORDER:
            x_copy(0, dx).start()

        @pl.when(k == 1)
        def _():
            reduce_send(0, 0)

        @pl.when(k == 0)
        def _():
            plan_copy.wait()
            blocks_copy.wait()

        acc[...] = jnp.zeros((GROUP * SIDE, SIDE), F32)
        chunk = slots // 8
        for i, d in enumerate(Z_ORDER):

            @pl.when(k == 0)
            def _():
                compact_from(i * chunk, chunk)

            z_copy(d).wait_recv()
            for dx in X_ORDER:
                x_copy(d, dx).start()

        @pl.when(k == 0)
        def _():
            compact_from(7 * chunk, slots - 7 * chunk)

        @pl.when(k == 1)
        def _():
            ar_own[0, 1] = reduce_take(0, 0)
            reduce_send(0, 1)

        for d in D_ORDER:
            for dx in X_ORDER:
                x_copy(d, dx).wait_recv()
            relay(d).start()

            @pl.when(k == 0)
            def _():
                densify(d)

            acc[...] += jnp.dot(
                dense[d], gat[p, d * NX : d * NX + NX].reshape(NX * SIDE, SIDE), preferred_element_type=F32
            )
        for d in D_ORDER:

            @pl.when(k == 0)
            def _():
                densify(NZ + d)

            relay(d).wait_recv()
            acc[...] += jnp.dot(
                dense[NZ + d], gat[p, 32 + d * NX : 32 + d * NX + NX].reshape(NX * SIDE, SIDE),
                preferred_element_type=F32,
            )

        part[p] = acc[...].astype(BF16).reshape(GROUP, SIDE, SIDE)

        def part_copy(dy):
            return remote(part.at[p, (y + dy) % NY], got.at[p, dy], ps.at[p], pr.at[p, dy], device(z, x, core, y + dy))

        for dy in (2, 1, 3):
            part_copy(dy).start()
        sent = gat.at[p, pl.ds(0, 63)]
        pltpu.make_async_copy(sent, sent, gs.at[p]).wait()

        @pl.when(k == 1)
        def _():
            sums = reduce_take(0, 1)
            theta[...] = jnp.broadcast_to(DAMPING - sums[0:1] / sums[1:2], (8, SIDE))

        own = acc[pl.ds(pl.multiple_of(y * SIDE, SIDE), SIDE), :]
        for dy in (1, 3, 2):
            part_copy(dy).wait_recv()
            own = own + got[p, dy].astype(F32)
        full = 2.0 * own
        unit = point[...]
        lean = row_sum(unit * full)
        flat = full - lean * unit
        lam[...] = jnp.where(k == 0, jnp.broadcast_to(lean, (SIDE, SIDE)), lam[...])
        before = vs[jnp.maximum(k - 1, 0)]
        new = jnp.where(k == 0, -flat, flat + (DAMPING - theta[0:1, :] - lam[...]) * before)
        vs[k] = new
        gat[1 - p, 0] = new.astype(BF16)

        @pl.when(k == 0)
        def _():
            square = new * new
            rows = jnp.concatenate(
                [jnp.sum(lam[...] * square, axis=0, keepdims=True), jnp.sum(square, axis=0, keepdims=True),
                 jnp.zeros((14, SIDE), F32)], axis=0)
            ar_own[0, 0] = jnp.broadcast_to(row_sum(rows), (16, SIDE))

        sent2 = part.at[p, pl.ds(0, 3)]
        pltpu.make_async_copy(sent2, sent2, ps.at[p]).wait()
        return carry

    def compact_from(start, count):
        total = compact(start, count)(total_get())
        out_res[...] = total

    def total_get():
        return out_res[...]

    out_res[...] = jnp.zeros((SIDE, SIDE), F32)
    lax.fori_loop(0, ITERS + 1, product, 0)

    grams = [jnp.sum(vs[i] * vs[j], axis=0, keepdims=True) for i, j in PAIRS]
    rows = jnp.concatenate(grams + [jnp.zeros((16 - len(PAIRS), SIDE), F32)], axis=0)
    ar_own[1, 0] = jnp.broadcast_to(row_sum(rows), (16, SIDE))
    reduce_send(1, 0)
    ar_own[1, 1] = reduce_take(1, 0)
    reduce_send(1, 1)
    total = reduce_take(1, 1)
    gram = {pair: total[e : e + 1, :] for e, pair in enumerate(PAIRS)}
    shift = theta[0:1, :]

    def dot(a, b):
        terms = [a[i] * b[j] * gram[(min(i, j), max(i, j))] for i in a for j in b]
        return functools.reduce(lambda s, t: s + t, terms)

    def axpy(a, scale, b):
        out = dict(a)
        for i, v in b.items():
            out[i] = out[i] + scale * v if i in out else scale * v
        return out

    one = jnp.ones((1, SIDE), F32)
    residual = {0: one}
    direction = {0: one}
    step = {}
    norm_now = dot(residual, residual)
    for turn in range(ITERS):
        image = {i + 1: v for i, v in direction.items()}
        image = axpy(image, shift, direction)
        alpha = norm_now / dot(direction, image)
        step = axpy(step, alpha, direction)
        residual = axpy(residual, -alpha, image)
        if turn < ITERS - 1:
            norm_next = dot(residual, residual)
            direction = axpy(residual, norm_next / norm_now, direction)
            norm_now = norm_next
    out_step[...] = functools.reduce(lambda s, t: s + t, [step[i] * vs[i] for i in sorted(step)])
    out_res[...] = functools.reduce(lambda s, t: s + t, [residual[i] * vs[i] for i in sorted(residual)])


def shards(y_prev, step_prev, accept, blocks, blk_row, blk_col):
    tiles = blocks[0, 0]
    slots = tiles.shape[0]
    vmem = pl.BlockSpec(memory_space=pltpu.VMEM)
    return pl.pallas_call(
        functools.partial(kernel, slots),
        out_shape=[jax.ShapeDtypeStruct(y_prev.shape, F32)] * 2,
        in_specs=[vmem, vmem, pl.BlockSpec(memory_space=pltpu.SMEM), vmem, vmem, pl.BlockSpec(memory_space=pl.ANY)],
        out_specs=[vmem, vmem],
        scratch_shapes=[
            pltpu.VMEM((slots, SIDE, SIDE), BF16),
            pltpu.VMEM((slots + 1, SIDE, SIDE), BF16),
            pltpu.VMEM((16, GROUP * SIDE, NX * SIDE), BF16),
            pltpu.VMEM((2, TILES, SIDE, SIDE), BF16),
            pltpu.VMEM((GROUP * SIDE, SIDE), F32),
            pltpu.VMEM((SIDE, SIDE), F32),
            pltpu.VMEM((SIDE, SIDE), F32),
            pltpu.VMEM((ITERS + 1, SIDE, SIDE), F32),
            pltpu.VMEM((2, GROUP, SIDE, SIDE), BF16),
            pltpu.VMEM((2, NY, SIDE, SIDE), BF16),
            pltpu.VMEM((2, 2, 16, SIDE), F32),
            pltpu.VMEM((2, 2, 16, 16, SIDE), F32),
            pltpu.VMEM((8, SIDE), F32),
            pltpu.VMEM((8, 256), I32),
            pltpu.SMEM((8, 256), I32),
            pltpu.SemaphoreType.DMA((2,)),
            pltpu.SemaphoreType.DMA((2,)),
            pltpu.SemaphoreType.DMA((2, NZ)),
            pltpu.SemaphoreType.DMA((2, NZ, NX)),
            pltpu.SemaphoreType.DMA((2, NZ)),
            pltpu.SemaphoreType.DMA((2,)),
            pltpu.SemaphoreType.DMA((2, NY)),
            pltpu.SemaphoreType.DMA((2, 2)),
            pltpu.SemaphoreType.DMA((2, 2)),
        ],
        compiler_params=pltpu.CompilerParams(
            collective_id=0, has_side_effects=True, vmem_limit_bytes=56 * 1024 * 1024
        ),
        cost_estimate=pl.CostEstimate(flops=4_300_000_000, bytes_accessed=7_000_000, transcendentals=128),
        name="trust_step",
    )(y_prev, step_prev, accept, blk_row[0], blk_col[0], tiles)


def solution(mesh):
    placed = (
        P(("row", "col"), None),
        P(("row", "col"), None),
        P(("row", "col")),
        P("row", "col", None, None, None),
        P("row", "col", None),
        P("row", "col", None),
    )
    return jax.shard_map(
        shards,
        mesh=mesh,
        in_specs=placed,
        out_specs=(P(("row", "col"), None), P(("row", "col"), None)),
        check_vma=False,
    )
```

time: 947 us -> 112 us (0.12)
  waiting for transfers between devices: 384 us -> 0 us
  blocking collectives: 381 us -> 0 us
  Pallas kernels: 0 us -> 107 us
  local copies, waits for them, and re-layouts: 77.4 us -> 2.95 us
  matrix products: 62 us -> 0 us
  between operations: 21.4 us -> 1.28 us
  other arithmetic: 18.7 us -> 0 us
    psum x5 -> x0, blocking collectives: 381 us -> none  [the longest x2 156 us: shards(): curv = lax.psum(jnp.sum(direction * image), ('row', 'col'))]
    all_gather x4 -> x0, waiting for transfers between devices: 310 us -> none  [apply_graph(): lax.all_gather(vector.astype(jnp.bfloat16), 'row', axis=0, tiled=True)]
    pallas_call x0 -> x1, Pallas kernels: none -> 107 us  [shards(): pl.pallas_call(functools.partial(kernel, slots), out_shape=[jax.ShapeDtyp...]
    reduce_scatter x4 -> x0, waiting for transfers between devices: 73.5 us -> none  [apply_graph(): lax.psum_scatter(partial_rows, 'col', scatter_dimension=0, tiled=True)]
    dot_general x8 -> x0, matrix products: 62 us -> none  [the longest x4 47.2 us: apply_graph(): jnp.einsum('sab,sbd->sad', tiles_own, tiles[cols_index], preferred_elemen...]
    dot_general x8 -> x0, local copies, waits for them, and re-layouts: 38.8 us -> none  [the longest x4 36 us: apply_graph(): jnp.einsum('sab,sbd->sad', tiles_own, tiles[cols_index], preferred_elemen...]
    gather x4 -> x0, local copies, waits for them, and re-layouts: 38.6 us -> none  [apply_graph(): tiles[cols_index]]
    reduce_sum x10 -> x0, other arithmetic: 12.9 us -> none  [the longest x3 4.73 us: shards(): curv = lax.psum(jnp.sum(direction * image), ('row', 'col'))]
  transfers between devices with their start and end apart: 8 -> 0, of which waited for: 8 -> 0; matrix products, arithmetic and copies ran while one was open for 0% -> 0% of each run, Pallas kernels for 0% -> 0%
where the time goes in v1:
time: 112 us; the launch traced here: 111 us
  Pallas kernels  107 us (96%)
  local copies, waits for them, and re-layouts  2.95 us (3%)
  between operations  1.28 us (1%)
    pallas_call x1, Pallas kernels, shards(): pl.pallas_call(functools.partial(kernel, slots), out_shape=[jax.ShapeDtyp...  107 us
    unnamed x2, local copies, waits for them, and re-layouts  2.95 us

profile of v1, /device:TPU:1, one launch (start us, length us, event | category | flops | bytes accessed | tf_op | source)
XLA Modules:
  0.0 111.5 jit_solution(9027161167224930784)
XLA Ops:
  1.3 107.2 %trust_step.1 = (f32[128,128]{1,0:T(8,128)}, f32[128,128]{1,0:T(8,128)}) custom-call(f32[128,128]{1,0:T(8,128)} %y_ref.1, f32[128,128]{1,0:T(8,128)} %step_ref.1, s32[1]{0:T(128)S(6)} %copy.10.accept_ref, s32[1,192]{1,0:T(1,128)} %bitcast.4, s32[1,192]{1,0:T(1,128)} %bitcast.5, bf16[192,128,128]{2,1,0:T(8,128)(2,1)} %bitcast.3), custom_call_target="tpu_custom_call" | custom-call | flops 4300000256 | bytes 7000000 | tf_op jit(solution)/shard_map/trust_step/pallas_call | solution.py:302
  108.5 1.5 %copy.11 = f32[128,128]{1,0:T(8,128)} copy(f32[128,128]{1,0:T(8,128)} %get-tuple-element.4) | data formatting | bytes 131072
  110.0 1.5 %copy.12 = f32[128,128]{1,0:T(8,128)} copy(f32[128,128]{1,0:T(8,128)} %get-tuple-element.5) | data formatting | bytes 131072

commit v2 on v1

--- a/solution.py
+++ b/solution.py
@@ -13,8 +13,12 @@
 NZ, NX, NY = 8, 4, 4
 SIDE = 128
 GROUP = 4
-TILES = 64
+TILES = 32
+UPPER = 96
+LOWER = SIDE - UPPER
 Z_ORDER = (1, 7, 2, 6, 3, 5, 4)
+LOW_ORDER = (1, 7, 2, 6, 3, 5, 4)
+LATE = 1
 X_ORDER = (2, 1, 3)
 D_ORDER = (0,) + Z_ORDER
 PAIRS = ((0, 0), (0, 1), (0, 2), (1, 1), (1, 2), (2, 2), (0, 3), (1, 3), (2, 3))
@@ -58,21 +62,22 @@
 
 def kernel(
     slots, y_ref, step_ref, accept_ref, row_ref, col_ref, blocks_ref, out_step, out_res,
-    raw, comp, dense, gat, acc, point, lam, vs, part, got, ar_own, ar_buf, theta, plan_v, plan_s,
-    local_sem, gs, zr, xr, cr, ps, pr, ars, arr,
+    raw, comp, dense, lent, gat, acc, acc_far, point, lam, vs, lean_rows, part, got, halves, ar_own, ar_buf, theta, plan_v, plan_s,
+    local_sem, gs, zr, br, xr, lent_s, lent_r, ws, wr, ps, pr, hs, hr, ars, arr,
 ):
     row = lax.axis_index("row")
     y = lax.axis_index("col")
     z, x, core = row // (2 * NX), row // 2 % NX, row % 2
 
-    first = [(dz, dk) for dz in range(NZ) for dk in range(2)]
-    second = [(dx, dy) for dx in range(NX) for dy in range(NY)]
-    peers = [[device(z + dz, x, core + dk, y) for dz, dk in first], [device(z, x + dx, core, y + dy) for dx, dy in second]]
+    first = [device(z + dz, x, core + dk, y) for dz in range(NZ) for dk in range(2)]
+    second = [device(z, x + dx, core, y + dy) for dx in range(NX) for dy in range(NY)]
+    owners = [device(z, x, core + j, y + dy) for j in range(2) for dy in range(NY)]
+    peers = (first, second)
+    greeted = first[1:] + second[1:] + owners[5:]
 
     barrier = pltpu.get_barrier_semaphore()
-    for stage in range(2):
-        for peer in peers[stage][1:]:
-            pl.semaphore_signal(barrier, inc=1, device_id=peer, device_id_type=MESH)
+    for peer in greeted:
+        pl.semaphore_signal(barrier, inc=1, device_id=peer, device_id_type=MESH)
     blocks_copy = pltpu.make_async_copy(blocks_ref, raw, local_sem.at[0])
     blocks_copy.start()
 
@@ -83,16 +88,20 @@
     vs[0] = jnp.zeros((SIDE, SIDE), F32)
     lam[...] = jnp.zeros((SIDE, SIDE), F32)
     theta[...] = jnp.zeros((8, SIDE), F32)
+    out_res[...] = jnp.zeros((SIDE, SIDE), F32)
     plan_v[...] = slot_plan(row_ref[...], col_ref[...], z, x, core)
     plan_copy = pltpu.make_async_copy(plan_v, plan_s, local_sem.at[1])
     plan_copy.start()
     comp[slots] = jnp.zeros((SIDE, SIDE), BF16)
-    pl.semaphore_wait(barrier, len(first) + len(second) - 2)
+    pl.semaphore_wait(barrier, len(greeted))
 
     def remote(src, dst, send, recv, peer):
         return pltpu.make_async_remote_copy(
             src_ref=src, dst_ref=dst, send_sem=send, recv_sem=recv, device_id=peer, device_id_type=MESH
         )
+
+    def settle(ref, sem):
+        pltpu.make_async_copy(ref, ref, sem).wait()
 
     def reduce_send(use, stage):
         for j in range(1, 16):
@@ -101,56 +110,79 @@
             ).start()
 
     def reduce_take(use, stage):
-        for sem in (arr, ars):
-            whole = ar_buf.at[use, stage, pl.ds(1, 15)]
-            pltpu.make_async_copy(whole, whole, sem.at[use, stage]).wait()
+        settle(ar_buf.at[use, stage, pl.ds(1, 15)], arr.at[use, stage])
         return ar_own[use, stage] + jnp.sum(ar_buf[use, stage, 1:16], axis=0)
 
     def compact(start, count):
         def one(j, total):
-            keep = plan_s[1, j].astype(F32)
-            total = keep * total + raw[plan_s[0, j]].astype(F32)
+            total = plan_s[1, j].astype(F32) * total + raw[plan_s[0, j]].astype(F32)
             comp[j] = total.astype(BF16)
             return total
 
-        return functools.partial(lax.fori_loop, start, start + count, one)
-
-    def densify(chunk):
-        def one(q, carry):
-            dx, r = q // GROUP, q % GROUP
-            dense[chunk, pl.ds(r * SIDE, SIDE), :] = jnp.concatenate(
-                [comp[plan_s[2, chunk * 16 + i * GROUP + r]] for i in range(NX)], axis=1
+        out_res[...] = lax.fori_loop(start, start + count, one, out_res[...])
+
+    def densify(chunk, store):
+        def one(r, carry):
+            store(
+                pl.multiple_of(r * SIDE, SIDE),
+                jnp.concatenate([comp[plan_s[2, chunk * 16 + i * GROUP + r]] for i in range(NX)], axis=1),
             )
             return carry
 
-        def rows(r, carry):
-            return one(r, carry)
-
-        lax.fori_loop(0, GROUP, rows, 0)
+        lax.fori_loop(0, GROUP, one, 0)
+
+    def lend(d):
+        return remote(lent.at[d], dense.at[d, pl.ds(GROUP * SIDE, GROUP * SIDE)], lent_s, lent_r.at[d], owners[NY])
 
     def product(k, carry):
         p = k % 2
 
         def tile(d, dx):
-            return gat.at[p, d * NX + dx]
+            return gat.at[p, d * NX + dx, pl.ds(0, UPPER)]
+
+        def low(d, dx, count):
+            return gat.at[p, pl.ds(d * NX + dx, count), pl.ds(UPPER, LOWER)]
 
         def z_copy(d):
             return remote(tile(0, 0), tile(d, 0), gs.at[p], zr.at[p, d], device(z + d, x, core, y))
 
         def x_copy(d, dx):
-            return remote(tile(d, 0), tile(d, dx), gs.at[p], xr.at[p, d, dx], device(z, x + dx, core, y))
-
-        def relay(d):
-            return remote(
-                gat.at[p, pl.ds(d * NX, NX)], gat.at[p, pl.ds(32 + d * NX, NX)], gs.at[p], cr.at[p, d],
-                device(z, x, core + 1, y),
+            return remote(tile(d, 0), tile(d, dx), gs.at[p], xr.at[p, d], device(z, x + dx, core, y))
+
+        def low_x_copy(dx):
+            return remote(low(0, 0, 1), low(0, dx, 1), gs.at[p], br.at[p, dx], device(z, x + dx, core, y))
+
+        def low_z_copy(d):
+            return remote(low(0, 0, NX), low(d, 0, NX), gs.at[p], xr.at[p, d], device(z + d, x, core, y))
+
+        def part_copy(o):
+            return remote(part.at[p, (y + o) % NY], got.at[p, o], ps.at[p], pr.at[p], owners[o])
+
+        def core_copy():
+            return remote(halves.at[p, 0], halves.at[p, 1], hs.at[p], hr.at[p], owners[NY])
+
+        def multiply(total, at, d, fresh):
+            term = jnp.dot(
+                dense[d, at : at + GROUP * SIDE],
+                gat[p, d * NX : d * NX + NX].reshape(NX * SIDE, SIDE),
+                preferred_element_type=F32,
             )
+            total[...] = term if fresh else total[...] + term
 
         for d in Z_ORDER:
             z_copy(d).start()
+        for dx in (1, 3, 2):
+            low_x_copy(dx).start()
         for dx in X_ORDER:
             x_copy(0, dx).start()
 
+        @pl.when(k >= 1)
+        def _():
+            settle(part.at[1 - p, pl.ds(0, 3)], ps.at[1 - p])
+            settle(halves.at[1 - p, 0], hs.at[1 - p])
+            for o in range(1, 8):
+                remote(lean_rows.at[k - 1, 0], lean_rows.at[k - 1, o], ws.at[k - 1], wr.at[k - 1], owners[o]).start()
+
         @pl.when(k == 1)
         def _():
             reduce_send(0, 0)
@@ -159,61 +191,78 @@
         def _():
             plan_copy.wait()
             blocks_copy.wait()
-
-        acc[...] = jnp.zeros((GROUP * SIDE, SIDE), F32)
-        chunk = slots // 8
+            compact(0, 24)
+
+        for dx in (1, 3, 2):
+            low_x_copy(dx).wait_recv()
+        for d in LOW_ORDER:
+            low_z_copy(d).start()
         for i, d in enumerate(Z_ORDER):
 
             @pl.when(k == 0)
             def _():
-                compact_from(i * chunk, chunk)
+                compact(24 + 24 * i, 24)
 
             z_copy(d).wait_recv()
             for dx in X_ORDER:
                 x_copy(d, dx).start()
 
-        @pl.when(k == 0)
-        def _():
-            compact_from(7 * chunk, slots - 7 * chunk)
-
         @pl.when(k == 1)
         def _():
             ar_own[0, 1] = reduce_take(0, 0)
             reduce_send(0, 1)
 
-        for d in D_ORDER:
-            for dx in X_ORDER:
-                x_copy(d, dx).wait_recv()
-            relay(d).start()
+        @pl.when(k == 0)
+        def _():
+            for d in D_ORDER:
+
+                def put(r, value):
+                    lent[d, pl.ds(r, SIDE), :] = value
+
+                densify(NZ + d, put)
+                lend(d).start()
+            for d in D_ORDER:
+
+                def keep(r, value):
+                    dense[d, pl.ds(r, SIDE), :] = value
+
+                densify(d, keep)
+
+        @pl.when(k == ITERS)
+        def _():
+            ar_own[1, 0] = local_grams()
+
+        for i, d in enumerate(D_ORDER):
+            rest = 3 * UPPER + (NX * LOWER if d else 0)
+            settle(gat.at[p, pl.ds(0, rest // 32), pl.ds(0, 32)], xr.at[p, d])
 
             @pl.when(k == 0)
             def _():
-                densify(d)
-
-            acc[...] += jnp.dot(
-                dense[d], gat[p, d * NX : d * NX + NX].reshape(NX * SIDE, SIDE), preferred_element_type=F32
-            )
-        for d in D_ORDER:
-
-            @pl.when(k == 0)
-            def _():
-                densify(NZ + d)
-
-            relay(d).wait_recv()
-            acc[...] += jnp.dot(
-                dense[NZ + d], gat[p, 32 + d * NX : 32 + d * NX + NX].reshape(NX * SIDE, SIDE),
-                preferred_element_type=F32,
-            )
-
-        part[p] = acc[...].astype(BF16).reshape(GROUP, SIDE, SIDE)
-
-        def part_copy(dy):
-            return remote(part.at[p, (y + dy) % NY], got.at[p, dy], ps.at[p], pr.at[p, dy], device(z, x, core, y + dy))
-
-        for dy in (2, 1, 3):
-            part_copy(dy).start()
-        sent = gat.at[p, pl.ds(0, 63)]
-        pltpu.make_async_copy(sent, sent, gs.at[p]).wait()
+                lend(d).wait_recv()
+
+            multiply(acc_far, GROUP * SIDE, d, i == 0)
+            if i < NZ - LATE:
+                multiply(acc, 0, d, i == 0)
+
+        for r in range(GROUP):
+            halves[p, 0, r] = acc_far[r * SIDE : (r + 1) * SIDE, :].astype(BF16)
+        core_copy().start()
+        for d in D_ORDER[NZ - LATE :]:
+            multiply(acc, 0, d, False)
+
+        @pl.when(k == ITERS)
+        def _():
+            ar_own[1, 0] = ar_own[1, 0] + far_grams()
+            reduce_send(1, 0)
+
+        core_copy().wait_recv()
+        for r in range(GROUP):
+            both = acc[r * SIDE : (r + 1) * SIDE, :] + halves[p, 1, r].astype(F32)
+            acc[r * SIDE : (r + 1) * SIDE, :] = both
+            part[p, r] = both.astype(BF16)
+        for o in (2, 1, 3):
+            part_copy(o).start()
+        settle(gat.at[p, pl.ds(0, 31)], gs.at[p])
 
         @pl.when(k == 1)
         def _():
@@ -221,9 +270,9 @@
             theta[...] = jnp.broadcast_to(DAMPING - sums[0:1] / sums[1:2], (8, SIDE))
 
         own = acc[pl.ds(pl.multiple_of(y * SIDE, SIDE), SIDE), :]
-        for dy in (1, 3, 2):
-            part_copy(dy).wait_recv()
-            own = own + got[p, dy].astype(F32)
+        settle(got.at[p, pl.ds(1, 3)], pr.at[p])
+        for o in range(1, NY):
+            own = own + got[p, o].astype(F32)
         full = 2.0 * own
         unit = point[...]
         lean = row_sum(unit * full)
@@ -234,32 +283,41 @@
         vs[k] = new
         gat[1 - p, 0] = new.astype(BF16)
 
+        @pl.when(k < ITERS)
+        def _():
+            lean_rows[k, 0] = (new - row_sum(unit * new) * unit).astype(BF16)
+
         @pl.when(k == 0)
         def _():
             square = new * new
-            rows = jnp.concatenate(
-                [jnp.sum(lam[...] * square, axis=0, keepdims=True), jnp.sum(square, axis=0, keepdims=True),
-                 jnp.zeros((14, SIDE), F32)], axis=0)
-            ar_own[0, 0] = jnp.broadcast_to(row_sum(rows), (16, SIDE))
-
-        sent2 = part.at[p, pl.ds(0, 3)]
-        pltpu.make_async_copy(sent2, sent2, ps.at[p]).wait()
+            ar_own[0, 0] = lane_sums([lam[...] * square, square])
+            settle(lent, lent_s)
+
         return carry
 
-    def compact_from(start, count):
-        total = compact(start, count)(total_get())
-        out_res[...] = total
-
-    def total_get():
-        return out_res[...]
-
-    out_res[...] = jnp.zeros((SIDE, SIDE), F32)
+    def lane_sums(terms):
+        rows = [jnp.sum(term, axis=0, keepdims=True) for term in terms]
+        rows.append(jnp.zeros((16 - len(rows), SIDE), F32))
+        return jnp.broadcast_to(row_sum(jnp.concatenate(rows, axis=0)), (16, SIDE))
+
+    def local_grams():
+        pull = (DAMPING - theta[0:1, :] - lam[...]) * vs[2]
+        return lane_sums([vs[i] * (vs[j] if j < ITERS else pull) for i, j in PAIRS])
+
+    def far_grams():
+        sums = [jnp.zeros((SIDE, SIDE), F32)] * ITERS
+        for i in range(ITERS):
+            settle(lean_rows.at[i, pl.ds(1, 7)], wr.at[i])
+        for b in range(2 * GROUP):
+            block = 2.0 * (acc, acc_far)[b // GROUP][b % GROUP * SIDE : (b % GROUP + 1) * SIDE, :]
+            o = b // GROUP * NY + (y + NY - b % GROUP) % NY
+            for i in range(ITERS):
+                sums[i] = sums[i] + lean_rows[i, o].astype(F32) * block
+        zero = jnp.zeros((SIDE, SIDE), F32)
+        return lane_sums([zero if j < ITERS else sums[i] for i, j in PAIRS])
+
     lax.fori_loop(0, ITERS + 1, product, 0)
 
-    grams = [jnp.sum(vs[i] * vs[j], axis=0, keepdims=True) for i, j in PAIRS]
-    rows = jnp.concatenate(grams + [jnp.zeros((16 - len(PAIRS), SIDE), F32)], axis=0)
-    ar_own[1, 0] = jnp.broadcast_to(row_sum(rows), (16, SIDE))
-    reduce_send(1, 0)
     ar_own[1, 1] = reduce_take(1, 0)
     reduce_send(1, 1)
     total = reduce_take(1, 1)
@@ -294,6 +352,14 @@
     out_step[...] = functools.reduce(lambda s, t: s + t, [step[i] * vs[i] for i in sorted(step)])
     out_res[...] = functools.reduce(lambda s, t: s + t, [residual[i] * vs[i] for i in sorted(residual)])
 
+    settle(part.at[1, pl.ds(0, 3)], ps.at[1])
+    settle(halves.at[1, 0], hs.at[1])
+    for i in range(ITERS):
+        settle(lean_rows.at[i, pl.ds(1, 7)], ws.at[i])
+    for use in range(2):
+        for stage in range(2):
+            settle(ar_buf.at[use, stage, pl.ds(1, 15)], ars.at[use, stage])
+
 
 def shards(y_prev, step_prev, accept, blocks, blk_row, blk_col):
     tiles = blocks[0, 0]
@@ -307,14 +373,18 @@
         scratch_shapes=[
             pltpu.VMEM((slots, SIDE, SIDE), BF16),
             pltpu.VMEM((slots + 1, SIDE, SIDE), BF16),
-            pltpu.VMEM((16, GROUP * SIDE, NX * SIDE), BF16),
+            pltpu.VMEM((NZ, 2 * GROUP * SIDE, NX * SIDE), BF16),
+            pltpu.VMEM((NZ, GROUP * SIDE, NX * SIDE), BF16),
             pltpu.VMEM((2, TILES, SIDE, SIDE), BF16),
+            pltpu.VMEM((GROUP * SIDE, SIDE), F32),
             pltpu.VMEM((GROUP * SIDE, SIDE), F32),
             pltpu.VMEM((SIDE, SIDE), F32),
             pltpu.VMEM((SIDE, SIDE), F32),
             pltpu.VMEM((ITERS + 1, SIDE, SIDE), F32),
+            pltpu.VMEM((ITERS, 2 * NY, SIDE, SIDE), BF16),
             pltpu.VMEM((2, GROUP, SIDE, SIDE), BF16),
             pltpu.VMEM((2, NY, SIDE, SIDE), BF16),
+            pltpu.VMEM((2, 2, GROUP, SIDE, SIDE), BF16),
             pltpu.VMEM((2, 2, 16, SIDE), F32),
             pltpu.VMEM((2, 2, 16, 16, SIDE), F32),
             pltpu.VMEM((8, SIDE), F32),
@@ -323,10 +393,16 @@
             pltpu.SemaphoreType.DMA((2,)),
             pltpu.SemaphoreType.DMA((2,)),
             pltpu.SemaphoreType.DMA((2, NZ)),
-            pltpu.SemaphoreType.DMA((2, NZ, NX)),
+            pltpu.SemaphoreType.DMA((2, NX)),
             pltpu.SemaphoreType.DMA((2, NZ)),
-            pltpu.SemaphoreType.DMA((2,)),
-            pltpu.SemaphoreType.DMA((2, NY)),
+            pltpu.SemaphoreType.DMA,
+            pltpu.SemaphoreType.DMA((NZ,)),
+            pltpu.SemaphoreType.DMA((ITERS,)),
+            pltpu.SemaphoreType.DMA((ITERS,)),
+            pltpu.SemaphoreType.DMA((2,)),
+            pltpu.SemaphoreType.DMA((2,)),
+            pltpu.SemaphoreType.DMA((2,)),
+            pltpu.SemaphoreType.DMA((2,)),
             pltpu.SemaphoreType.DMA((2, 2)),
             pltpu.SemaphoreType.DMA((2, 2)),
         ],

time: 112 us -> 103 us (0.920)
  Pallas kernels: 107 us -> 98.7 us
    pallas_call x1, Pallas kernels: 107 us -> 98.7 us  [shards(): pl.pallas_call(functools.partial(kernel, slots), out_shape=[jax.ShapeDtyp...]
where the time goes in v2:
time: 103 us
  Pallas kernels  98.7 us (96%)
  local copies, waits for them, and re-layouts  2.95 us (3%)
  between operations  1.28 us (1%)
    pallas_call x1, Pallas kernels, shards(): pl.pallas_call(functools.partial(kernel, slots), out_shape=[jax.ShapeDtyp...  98.7 us
    unnamed x2, local copies, waits for them, and re-layouts  2.95 us

profile of v2, /device:TPU:1, one launch (start us, length us, event | category | flops | bytes accessed | tf_op | source)
XLA Modules:
  0.0 102.9 jit_solution(1084879247620845330)
XLA Ops:
  1.3 98.7 %trust_step.1 = (f32[128,128]{1,0:T(8,128)}, f32[128,128]{1,0:T(8,128)}) custom-call(f32[128,128]{1,0:T(8,128)} %y_ref.1, f32[128,128]{1,0:T(8,128)} %step_ref.1, s32[1]{0:T(128)S(6)} %copy.10.accept_ref, s32[1,192]{1,0:T(1,128)} %bitcast.4, s32[1,192]{1,0:T(1,128)} %bitcast.5, bf16[192,128,128]{2,1,0:T(8,128)(2,1)} %bitcast.3), custom_call_target="tpu_custom_call" | custom-call | flops 4300000256 | bytes 7000000 | tf_op jit(solution)/shard_map/trust_step/pallas_call | solution.py:368
  99.9 1.5 %copy.11 = f32[128,128]{1,0:T(8,128)} copy(f32[128,128]{1,0:T(8,128)} %get-tuple-element.4) | data formatting | bytes 131072
  101.4 1.5 %copy.12 = f32[128,128]{1,0:T(8,128)} copy(f32[128,128]{1,0:T(8,128)} %get-tuple-element.5) | data formatting | bytes 131072

commit v3 on v2

--- a/solution.py
+++ b/solution.py
@@ -16,11 +16,9 @@
 TILES = 32
 UPPER = 96
 LOWER = SIDE - UPPER
-Z_ORDER = (1, 7, 2, 6, 3, 5, 4)
-LOW_ORDER = (1, 7, 2, 6, 3, 5, 4)
-LATE = 1
+PLANES = (0, 1, 7, 2, 6, 3, 5, 4)
+RUNS = ((1, 2), (3, 2), (5, 2), (7, 1))
 X_ORDER = (2, 1, 3)
-D_ORDER = (0,) + Z_ORDER
 PAIRS = ((0, 0), (0, 1), (0, 2), (1, 1), (1, 2), (2, 2), (0, 3), (1, 3), (2, 3))
 F32 = jnp.float32
 BF16 = jnp.bfloat16
@@ -41,6 +39,7 @@
     col = jnp.concatenate([cols, jnp.zeros((1, 256 - slots), I32)], axis=1)
     lane = lax.broadcasted_iota(I32, (1, 256), 1)
     dz = (z + NZ - col // 8) % NZ
+    dz = jnp.where(dz == 0, 0, jnp.where(dz <= NZ // 2, 2 * dz - 1, 2 * (NZ - dz)))
     dx = (x + NX - (col // 2) % NX) % NX
     rel = (col + core) % 2
     key_row = jnp.where(lane < slots, ((rel * NZ + dz) * NX + dx) * GROUP + far, 1 << 12)
@@ -62,18 +61,21 @@
 
 def kernel(
     slots, y_ref, step_ref, accept_ref, row_ref, col_ref, blocks_ref, out_step, out_res,
-    raw, comp, dense, lent, gat, acc, acc_far, point, lam, vs, lean_rows, part, got, halves, ar_own, ar_buf, theta, plan_v, plan_s,
+    raw, comp, dense, lent, arrivals, gat, acc, acc_far, point, lam, vs, lean_rows, part, got, halves, ar_own, ar_buf, theta, plan_v, plan_s,
     local_sem, gs, zr, br, xr, lent_s, lent_r, ws, wr, ps, pr, hs, hr, ars, arr,
 ):
     row = lax.axis_index("row")
     y = lax.axis_index("col")
     z, x, core = row // (2 * NX), row // 2 % NX, row % 2
 
-    first = [device(z + dz, x, core + dk, y) for dz in range(NZ) for dk in range(2)]
-    second = [device(z, x + dx, core, y + dy) for dx in range(NX) for dy in range(NY)]
+    plane = [device(z + dz, x + dx, core, y) for dz in range(NZ) for dx in range(NX)]
     owners = [device(z, x, core + j, y + dy) for j in range(2) for dy in range(NY)]
-    peers = (first, second)
-    greeted = first[1:] + second[1:] + owners[5:]
+    peers = (plane, owners)
+    far_first = [
+        sorted(range(1, m * n), key=lambda j: -(min(j // n, m - j // n) + min(j % n, n - j % n)))
+        for m, n in ((NZ, NX), (2, NY))
+    ]
+    greeted = plane[1:] + owners[1:]
 
     barrier = pltpu.get_barrier_semaphore()
     for peer in greeted:
@@ -84,16 +86,16 @@
     moved = y_ref[...] + accept_ref[0].astype(F32) * step_ref[...]
     unit = moved * lax.rsqrt(row_sum(moved * moved) + 1e-06)
     point[...] = unit
-    gat[0, 0] = unit.astype(BF16)
+    gat[0, 0, 0] = unit.astype(BF16)
     vs[0] = jnp.zeros((SIDE, SIDE), F32)
     lam[...] = jnp.zeros((SIDE, SIDE), F32)
     theta[...] = jnp.zeros((8, SIDE), F32)
     out_res[...] = jnp.zeros((SIDE, SIDE), F32)
-    plan_v[...] = slot_plan(row_ref[...], col_ref[...], z, x, core)
     plan_copy = pltpu.make_async_copy(plan_v, plan_s, local_sem.at[1])
-    plan_copy.start()
     comp[slots] = jnp.zeros((SIDE, SIDE), BF16)
     pl.semaphore_wait(barrier, len(greeted))
+
+    diagonal = lax.broadcasted_iota(I32, (16, SIDE), 0) == lax.broadcasted_iota(I32, (16, SIDE), 1)
 
     def remote(src, dst, send, recv, peer):
         return pltpu.make_async_remote_copy(
@@ -104,14 +106,18 @@
         pltpu.make_async_copy(ref, ref, sem).wait()
 
     def reduce_send(use, stage):
-        for j in range(1, 16):
+        for j in far_first[stage]:
             remote(
                 ar_own.at[use, stage], ar_buf.at[use, stage, j], ars.at[use, stage], arr.at[use, stage], peers[stage][j]
             ).start()
 
     def reduce_take(use, stage):
-        settle(ar_buf.at[use, stage, pl.ds(1, 15)], arr.at[use, stage])
-        return ar_own[use, stage] + jnp.sum(ar_buf[use, stage, 1:16], axis=0)
+        count = len(peers[stage])
+        settle(ar_buf.at[use, stage, pl.ds(1, count - 1)], arr.at[use, stage])
+        return ar_own[use, stage] + jnp.sum(ar_buf[use, stage, 1:count], axis=0)
+
+    def spread(total):
+        return jnp.broadcast_to(row_sum(jnp.where(diagonal, jnp.broadcast_to(total, (16, SIDE)), 0.0)), (16, SIDE))
 
     def compact(start, count):
         def one(j, total):
@@ -137,139 +143,161 @@
     def product(k, carry):
         p = k % 2
 
-        def tile(d, dx):
-            return gat.at[p, d * NX + dx, pl.ds(0, UPPER)]
-
-        def low(d, dx, count):
-            return gat.at[p, pl.ds(d * NX + dx, count), pl.ds(UPPER, LOWER)]
-
-        def z_copy(d):
-            return remote(tile(0, 0), tile(d, 0), gs.at[p], zr.at[p, d], device(z + d, x, core, y))
-
-        def x_copy(d, dx):
-            return remote(tile(d, 0), tile(d, dx), gs.at[p], xr.at[p, d], device(z, x + dx, core, y))
+        def high(i, count, dx):
+            return gat.at[p, pl.ds(i, count), dx, pl.ds(0, UPPER)]
+
+        def low(i, dx, count):
+            return gat.at[p, i, pl.ds(dx, count), pl.ds(UPPER, LOWER)]
+
+        def z_copy(i):
+            return remote(high(0, 1, 0), high(i, 1, 0), gs.at[p], zr.at[p, i], device(z + PLANES[i], x, core, y))
+
+        def x_copy(i, count, dx):
+            return remote(high(i, count, 0), high(i, count, dx), gs.at[p], xr.at[p, i], device(z, x + dx, core, y))
 
         def low_x_copy(dx):
             return remote(low(0, 0, 1), low(0, dx, 1), gs.at[p], br.at[p, dx], device(z, x + dx, core, y))
 
-        def low_z_copy(d):
-            return remote(low(0, 0, NX), low(d, 0, NX), gs.at[p], xr.at[p, d], device(z + d, x, core, y))
+        def low_z_copy(i, run):
+            return remote(low(0, 0, NX), low(i, 0, NX), gs.at[p], xr.at[p, run], device(z + PLANES[i], x, core, y))
 
         def part_copy(o):
             return remote(part.at[p, (y + o) % NY], got.at[p, o], ps.at[p], pr.at[p], owners[o])
 
-        def core_copy():
-            return remote(halves.at[p, 0], halves.at[p, 1], hs.at[p], hr.at[p], owners[NY])
-
-        def multiply(total, at, d, fresh):
-            term = jnp.dot(
-                dense[d, at : at + GROUP * SIDE],
-                gat[p, d * NX : d * NX + NX].reshape(NX * SIDE, SIDE),
-                preferred_element_type=F32,
+        def core_copy(dy):
+            r = (y + dy) % NY
+            return remote(halves.at[p, 0, r], halves.at[p, 1, r], hs.at[p], hr.at[p, dy], owners[NY])
+
+        def multiply(total, at, i, count):
+            term = functools.reduce(
+                lambda s, t: s + t,
+                [
+                    jnp.dot(
+                        dense[n, at : at + GROUP * SIDE],
+                        gat[p, n].reshape(NX * SIDE, SIDE),
+                        preferred_element_type=F32,
+                    )
+                    for n in range(i, i + count)
+                ],
             )
-            total[...] = term if fresh else total[...] + term
-
-        for d in Z_ORDER:
-            z_copy(d).start()
+            total[...] = total[...] + term if i else term
+
+        for i in range(1, NZ):
+            z_copy(i).start()
         for dx in (1, 3, 2):
             low_x_copy(dx).start()
         for dx in X_ORDER:
-            x_copy(0, dx).start()
+            x_copy(0, 1, dx).start()
 
         @pl.when(k >= 1)
         def _():
             settle(part.at[1 - p, pl.ds(0, 3)], ps.at[1 - p])
             settle(halves.at[1 - p, 0], hs.at[1 - p])
+            new = vs[k - 1]
+            lean_rows[k - 1, 0] = (new - row_sum(point[...] * new) * point[...]).astype(BF16)
+
+        @pl.when(k == 1)
+        def _():
+            square = vs[0] * vs[0]
+            ar_own[0, 0] = lane_sums([lam[...] * square, square])
+            reduce_send(0, 0)
+
+        @pl.when(k == 0)
+        def _():
+            plan_v[...] = slot_plan(row_ref[...], col_ref[...], z, x, core)
+            plan_copy.start()
+
+        for dx in (1, 3, 2):
+            low_x_copy(dx).wait_recv()
+
+        @pl.when(k == 0)
+        def _():
+            plan_copy.wait()
+            blocks_copy.wait()
+
+        for n, (i, count) in enumerate(RUNS):
+
+            @pl.when(k == 0)
+            def _():
+                compact(48 * n, 48)
+
+            for m in range(count):
+                z_copy(i + m).wait_recv()
+            for dx in X_ORDER:
+                x_copy(i, count, dx).start()
+            if n == 0:
+                for m in range(1, NZ):
+                    low_z_copy(m, next(i0 for i0, c in RUNS if i0 <= m < i0 + c)).start()
+
+        @pl.when(k >= 1)
+        def _():
             for o in range(1, 8):
                 remote(lean_rows.at[k - 1, 0], lean_rows.at[k - 1, o], ws.at[k - 1], wr.at[k - 1], owners[o]).start()
 
         @pl.when(k == 1)
         def _():
-            reduce_send(0, 0)
+            ar_own[0, 1] = reduce_take(0, 0)
+            reduce_send(0, 1)
 
         @pl.when(k == 0)
         def _():
-            plan_copy.wait()
-            blocks_copy.wait()
-            compact(0, 24)
-
-        for dx in (1, 3, 2):
-            low_x_copy(dx).wait_recv()
-        for d in LOW_ORDER:
-            low_z_copy(d).start()
-        for i, d in enumerate(Z_ORDER):
+            for i in range(NZ):
+
+                def put(r, value):
+                    lent[i, pl.ds(r, SIDE), :] = value
+
+                densify(NZ + i, put)
+                lend(i).start()
+            for i in range(NZ):
+
+                def keep(r, value):
+                    dense[i, pl.ds(r, SIDE), :] = value
+
+                densify(i, keep)
+
+        @pl.when(k == ITERS)
+        def _():
+            ar_own[1, 0] = local_grams()
+
+        for i, count in ((0, 1),) + RUNS:
+            rest = count * (3 * UPPER + (NX * LOWER if i else 0)) // 32
+            settle(arrivals.at[pl.ds(0, rest)], xr.at[p, i])
 
             @pl.when(k == 0)
             def _():
-                compact(24 + 24 * i, 24)
-
-            z_copy(d).wait_recv()
-            for dx in X_ORDER:
-                x_copy(d, dx).start()
-
-        @pl.when(k == 1)
-        def _():
-            ar_own[0, 1] = reduce_take(0, 0)
-            reduce_send(0, 1)
-
-        @pl.when(k == 0)
-        def _():
-            for d in D_ORDER:
-
-                def put(r, value):
-                    lent[d, pl.ds(r, SIDE), :] = value
-
-                densify(NZ + d, put)
-                lend(d).start()
-            for d in D_ORDER:
-
-                def keep(r, value):
-                    dense[d, pl.ds(r, SIDE), :] = value
-
-                densify(d, keep)
-
-        @pl.when(k == ITERS)
-        def _():
-            ar_own[1, 0] = local_grams()
-
-        for i, d in enumerate(D_ORDER):
-            rest = 3 * UPPER + (NX * LOWER if d else 0)
-            settle(gat.at[p, pl.ds(0, rest // 32), pl.ds(0, 32)], xr.at[p, d])
-
-            @pl.when(k == 0)
-            def _():
-                lend(d).wait_recv()
-
-            multiply(acc_far, GROUP * SIDE, d, i == 0)
-            if i < NZ - LATE:
-                multiply(acc, 0, d, i == 0)
-
-        for r in range(GROUP):
-            halves[p, 0, r] = acc_far[r * SIDE : (r + 1) * SIDE, :].astype(BF16)
-        core_copy().start()
-        for d in D_ORDER[NZ - LATE :]:
-            multiply(acc, 0, d, False)
+                for n in range(i, i + count):
+                    lend(n).wait_recv()
+
+            multiply(acc_far, GROUP * SIDE, i, count)
+            if i != RUNS[-1][0]:
+                multiply(acc, 0, i, count)
+
+        for dy in (2, 1, 3, 0):
+            r = (y + dy) % NY
+            halves[p, 0, r] = acc_far[pl.ds(pl.multiple_of(r * SIDE, SIDE), SIDE), :].astype(BF16)
+            core_copy(dy).start()
+        multiply(acc, 0, *RUNS[-1])
 
         @pl.when(k == ITERS)
         def _():
             ar_own[1, 0] = ar_own[1, 0] + far_grams()
             reduce_send(1, 0)
 
-        core_copy().wait_recv()
-        for r in range(GROUP):
-            both = acc[r * SIDE : (r + 1) * SIDE, :] + halves[p, 1, r].astype(F32)
-            acc[r * SIDE : (r + 1) * SIDE, :] = both
+        for dy in (2, 1, 3):
+            core_copy(dy).wait_recv()
+            r = (y + dy) % NY
+            both = acc[pl.ds(pl.multiple_of(r * SIDE, SIDE), SIDE), :] + halves[p, 1, r].astype(F32)
             part[p, r] = both.astype(BF16)
-        for o in (2, 1, 3):
-            part_copy(o).start()
-        settle(gat.at[p, pl.ds(0, 31)], gs.at[p])
+            part_copy(dy).start()
+        core_copy(0).wait_recv()
+        settle(arrivals.at[pl.ds(0, 31 * NX)], gs.at[p])
 
         @pl.when(k == 1)
         def _():
-            sums = reduce_take(0, 1)
+            sums = spread(reduce_take(0, 1))
             theta[...] = jnp.broadcast_to(DAMPING - sums[0:1] / sums[1:2], (8, SIDE))
 
-        own = acc[pl.ds(pl.multiple_of(y * SIDE, SIDE), SIDE), :]
+        own = acc[pl.ds(pl.multiple_of(y * SIDE, SIDE), SIDE), :] + halves[p, 1, y].astype(F32)
         settle(got.at[p, pl.ds(1, 3)], pr.at[p])
         for o in range(1, NY):
             own = own + got[p, o].astype(F32)
@@ -281,16 +309,10 @@
         before = vs[jnp.maximum(k - 1, 0)]
         new = jnp.where(k == 0, -flat, flat + (DAMPING - theta[0:1, :] - lam[...]) * before)
         vs[k] = new
-        gat[1 - p, 0] = new.astype(BF16)
-
-        @pl.when(k < ITERS)
-        def _():
-            lean_rows[k, 0] = (new - row_sum(unit * new) * unit).astype(BF16)
+        gat[1 - p, 0, 0] = new.astype(BF16)
 
         @pl.when(k == 0)
         def _():
-            square = new * new
-            ar_own[0, 0] = lane_sums([lam[...] * square, square])
             settle(lent, lent_s)
 
         return carry
@@ -298,7 +320,8 @@
     def lane_sums(terms):
         rows = [jnp.sum(term, axis=0, keepdims=True) for term in terms]
         rows.append(jnp.zeros((16 - len(rows), SIDE), F32))
-        return jnp.broadcast_to(row_sum(jnp.concatenate(rows, axis=0)), (16, SIDE))
+        sums = jnp.broadcast_to(row_sum(jnp.concatenate(rows, axis=0)), (16, SIDE))
+        return jnp.sum(jnp.where(diagonal, sums, 0.0), axis=0, keepdims=True)
 
     def local_grams():
         pull = (DAMPING - theta[0:1, :] - lam[...]) * vs[2]
@@ -320,7 +343,7 @@
 
     ar_own[1, 1] = reduce_take(1, 0)
     reduce_send(1, 1)
-    total = reduce_take(1, 1)
+    total = spread(reduce_take(1, 1))
     gram = {pair: total[e : e + 1, :] for e, pair in enumerate(PAIRS)}
     shift = theta[0:1, :]
 
@@ -358,14 +381,19 @@
         settle(lean_rows.at[i, pl.ds(1, 7)], ws.at[i])
     for use in range(2):
         for stage in range(2):
-            settle(ar_buf.at[use, stage, pl.ds(1, 15)], ars.at[use, stage])
+            settle(ar_buf.at[use, stage, pl.ds(1, len(peers[stage]) - 1)], ars.at[use, stage])
+
+
+def finish(step_ref, res_ref, out_step, out_res):
+    out_step[...] = step_ref[...]
+    out_res[...] = res_ref[...]
 
 
 def shards(y_prev, step_prev, accept, blocks, blk_row, blk_col):
     tiles = blocks[0, 0]
     slots = tiles.shape[0]
     vmem = pl.BlockSpec(memory_space=pltpu.VMEM)
-    return pl.pallas_call(
+    both = pl.pallas_call(
         functools.partial(kernel, slots),
         out_shape=[jax.ShapeDtypeStruct(y_prev.shape, F32)] * 2,
         in_specs=[vmem, vmem, pl.BlockSpec(memory_space=pltpu.SMEM), vmem, vmem, pl.BlockSpec(memory_space=pl.ANY)],
@@ -375,7 +403,8 @@
             pltpu.VMEM((slots + 1, SIDE, SIDE), BF16),
             pltpu.VMEM((NZ, 2 * GROUP * SIDE, NX * SIDE), BF16),
             pltpu.VMEM((NZ, GROUP * SIDE, NX * SIDE), BF16),
-            pltpu.VMEM((2, TILES, SIDE, SIDE), BF16),
+            pltpu.VMEM((TILES * NX, SIDE // NX, SIDE), BF16),
+            pltpu.VMEM((2, NZ, NX, SIDE, SIDE), BF16),
             pltpu.VMEM((GROUP * SIDE, SIDE), F32),
             pltpu.VMEM((GROUP * SIDE, SIDE), F32),
             pltpu.VMEM((SIDE, SIDE), F32),
@@ -385,8 +414,8 @@
             pltpu.VMEM((2, GROUP, SIDE, SIDE), BF16),
             pltpu.VMEM((2, NY, SIDE, SIDE), BF16),
             pltpu.VMEM((2, 2, GROUP, SIDE, SIDE), BF16),
-            pltpu.VMEM((2, 2, 16, SIDE), F32),
-            pltpu.VMEM((2, 2, 16, 16, SIDE), F32),
+            pltpu.VMEM((2, 2, 1, SIDE), F32),
+            pltpu.VMEM((2, 2, NZ * NX, 1, SIDE), F32),
             pltpu.VMEM((8, SIDE), F32),
             pltpu.VMEM((8, 256), I32),
             pltpu.SMEM((8, 256), I32),
@@ -402,7 +431,7 @@
             pltpu.SemaphoreType.DMA((2,)),
             pltpu.SemaphoreType.DMA((2,)),
             pltpu.SemaphoreType.DMA((2,)),
-            pltpu.SemaphoreType.DMA((2,)),
+            pltpu.SemaphoreType.DMA((2, NY)),
             pltpu.SemaphoreType.DMA((2, 2)),
             pltpu.SemaphoreType.DMA((2, 2)),
         ],
@@ -412,6 +441,13 @@
         cost_estimate=pl.CostEstimate(flops=4_300_000_000, bytes_accessed=7_000_000, transcendentals=128),
         name="trust_step",
     )(y_prev, step_prev, accept, blk_row[0], blk_col[0], tiles)
+    return pl.pallas_call(
+        finish,
+        out_shape=[jax.ShapeDtypeStruct(y_prev.shape, F32)] * 2,
+        in_specs=[vmem, vmem],
+        out_specs=[vmem, vmem],
+        name="finish",
+    )(*both)
 
 
 def solution(mesh):

time: 103 us -> 98.2 us (0.953)
  local copies, waits for them, and re-layouts: 2.95 us -> 0 us
  Pallas kernels: 98.7 us -> 96.7 us
    pallas_call x1, Pallas kernels: 98.7 us -> 95.2 us  [shards(): pl.pallas_call(functools.partial(kernel, slots), out_shape=[jax.ShapeDtyp...]
    unnamed x2 -> x0, local copies, waits for them, and re-layouts: 2.95 us -> none
    pallas_call x0 -> x1, Pallas kernels: none -> 1.53 us  [shards(): pl.pallas_call(finish, out_shape=[jax.ShapeDtypeStruct(y_prev.shape, F32)...]
where the time goes in v3:
time: 98.2 us; the launch traced here: 98 us
  Pallas kernels  96.7 us (98%)
  between operations  1.28 us (1%)
    pallas_call x1, Pallas kernels, shards(): pl.pallas_call(functools.partial(kernel, slots), out_shape=[jax.ShapeDtyp...  95.2 us

profile of v3, /device:TPU:1, one launch (start us, length us, event | category | flops | bytes accessed | tf_op | source)
XLA Modules:
  0.0 98.0 jit_solution(15668088568437531965)
XLA Ops:
  1.3 95.2 %trust_step.1 = (f32[128,128]{1,0:T(8,128)}, f32[128,128]{1,0:T(8,128)}) custom-call(f32[128,128]{1,0:T(8,128)} %y_ref.1, f32[128,128]{1,0:T(8,128)} %step_ref.1, s32[1]{0:T(128)S(6)} %copy.8.accept_ref, s32[1,192]{1,0:T(1,128)} %bitcast.4, s32[1,192]{1,0:T(1,128)} %bitcast.5, bf16[192,128,128]{2,1,0:T(8,128)(2,1)} %bitcast.3), custom_call_target="tpu_custom_call" | custom-call | flops 4300000256 | bytes 7000000 | tf_op jit(solution)/shard_map/trust_step/pallas_call | solution.py:396
  96.5 1.5 %finish.1 = (f32[128,128]{1,0:T(8,128)}, f32[128,128]{1,0:T(8,128)}) custom-call(f32[128,128]{1,0:T(8,128)} %get-tuple-element.4.step_ref, f32[128,128]{1,0:T(8,128)} %get-tuple-element.5.res_ref), custom_call_target="tpu_custom_call" | custom-call | tf_op jit(solution)/shard_map/finish/pallas_call | solution.py:444

commit v4 on v3

--- a/solution.py
+++ b/solution.py
@@ -60,8 +60,8 @@
 
 
 def kernel(
-    slots, y_ref, step_ref, accept_ref, row_ref, col_ref, blocks_ref, out_step, out_res,
-    raw, comp, dense, lent, arrivals, gat, acc, acc_far, point, lam, vs, lean_rows, part, got, halves, ar_own, ar_buf, theta, plan_v, plan_s,
+    slots, y_hbm, step_hbm, accept_hbm, row_hbm, col_hbm, blocks_ref, out_step, out_res,
+    y_ref, step_ref, accept_ref, row_ref, col_ref, raw, comp, dense, lent, arrivals, gat, acc, acc_far, point, lam, vs, lean_rows, part, got, halves, ar_own, ar_buf, theta, plan_v, plan_s,
     local_sem, gs, zr, br, xr, lent_s, lent_r, ws, wr, ps, pr, hs, hr, ars, arr,
 ):
     row = lax.axis_index("row")
@@ -75,15 +75,21 @@
         sorted(range(1, m * n), key=lambda j: -(min(j // n, m - j // n) + min(j % n, n - j % n)))
         for m, n in ((NZ, NX), (2, NY))
     ]
-    greeted = plane[1:] + owners[1:]
+    greeted = plane[1:NX] + plane[NX::NX] + owners[1:]
 
     barrier = pltpu.get_barrier_semaphore()
     for peer in greeted:
         pl.semaphore_signal(barrier, inc=1, device_id=peer, device_id_type=MESH)
+    pairs = ((y_hbm, y_ref), (step_hbm, step_ref), (accept_hbm, accept_ref), (row_hbm, row_ref), (col_hbm, col_ref))
+    small = [pltpu.make_async_copy(src, dst, local_sem.at[2 + n]) for n, (src, dst) in enumerate(pairs)]
+    for copy in small:
+        copy.start()
     blocks_copy = pltpu.make_async_copy(blocks_ref, raw, local_sem.at[0])
     blocks_copy.start()
-
-    moved = y_ref[...] + accept_ref[0].astype(F32) * step_ref[...]
+    for copy in small:
+        copy.wait()
+
+    moved = y_ref[...] + accept_ref[...].astype(F32) * step_ref[...]
     unit = moved * lax.rsqrt(row_sum(moved * moved) + 1e-06)
     point[...] = unit
     gat[0, 0, 0] = unit.astype(BF16)
@@ -396,9 +402,14 @@
     both = pl.pallas_call(
         functools.partial(kernel, slots),
         out_shape=[jax.ShapeDtypeStruct(y_prev.shape, F32)] * 2,
-        in_specs=[vmem, vmem, pl.BlockSpec(memory_space=pltpu.SMEM), vmem, vmem, pl.BlockSpec(memory_space=pl.ANY)],
+        in_specs=[pl.BlockSpec(memory_space=pl.ANY)] * 6,
         out_specs=[vmem, vmem],
         scratch_shapes=[
+            pltpu.VMEM(y_prev.shape, F32),
+            pltpu.VMEM(y_prev.shape, F32),
+            pltpu.VMEM((1, 1), I32),
+            pltpu.VMEM((1, slots), I32),
+            pltpu.VMEM((1, slots), I32),
             pltpu.VMEM((slots, SIDE, SIDE), BF16),
             pltpu.VMEM((slots + 1, SIDE, SIDE), BF16),
             pltpu.VMEM((NZ, 2 * GROUP * SIDE, NX * SIDE), BF16),
@@ -419,7 +430,7 @@
             pltpu.VMEM((8, SIDE), F32),
             pltpu.VMEM((8, 256), I32),
             pltpu.SMEM((8, 256), I32),
-            pltpu.SemaphoreType.DMA((2,)),
+            pltpu.SemaphoreType.DMA((7,)),
             pltpu.SemaphoreType.DMA((2,)),
             pltpu.SemaphoreType.DMA((2, NZ)),
             pltpu.SemaphoreType.DMA((2, NX)),
@@ -440,7 +451,7 @@
         ),
         cost_estimate=pl.CostEstimate(flops=4_300_000_000, bytes_accessed=7_000_000, transcendentals=128),
         name="trust_step",
-    )(y_prev, step_prev, accept, blk_row[0], blk_col[0], tiles)
+    )(y_prev, step_prev, accept[None], blk_row[0], blk_col[0], tiles)
     return pl.pallas_call(
         finish,
         out_shape=[jax.ShapeDtypeStruct(y_prev.shape, F32)] * 2,

time: 98.2 us -> 96.4 us (0.982)
  Pallas kernels: 96.7 us -> 95 us
    pallas_call x1, Pallas kernels: 95.2 us -> 93.5 us  [shards(): pl.pallas_call(functools.partial(kernel, slots), out_shape=[jax.ShapeDtyp...]
where the time goes in v4:
time: 96.4 us; the launch traced here: 96.3 us
  Pallas kernels  95 us (99%)
  between operations  1.28 us (1%)
    pallas_call x1, Pallas kernels, shards(): pl.pallas_call(functools.partial(kernel, slots), out_shape=[jax.ShapeDtyp...  93.5 us

profile of v4, /device:TPU:1, one launch (start us, length us, event | category | flops | bytes accessed | tf_op | source)
XLA Modules:
  0.0 96.3 jit_solution(11690055498865120144)
XLA Ops:
  1.3 93.5 %trust_step.1 = (f32[128,128]{1,0:T(8,128)}, f32[128,128]{1,0:T(8,128)}) custom-call(f32[128,128]{1,0:T(8,128)} %y_hbm.1, f32[128,128]{1,0:T(8,128)} %step_hbm.1, s32[1,1]{1,0:T(1,128)} %bitcast.4.accept_hbm, s32[1,192]{1,0:T(1,128)} %bitcast.6, s32[1,192]{1,0:T(1,128)} %bitcast.7, bf16[192,128,128]{2,1,0:T(8,128)(2,1)} %bitcast.5), custom_call_target="tpu_custom_call" | custom-call | flops 4300000256 | bytes 7000000 | tf_op jit(solution)/shard_map/trust_step/pallas_call | solution.py:402
  94.7 1.5 %finish.1 = (f32[128,128]{1,0:T(8,128)}, f32[128,128]{1,0:T(8,128)}) custom-call(f32[128,128]{1,0:T(8,128)} %get-tuple-element.4.step_ref, f32[128,128]{1,0:T(8,128)} %get-tuple-element.5.res_ref), custom_call_target="tpu_custom_call" | custom-call | tf_op jit(solution)/shard_map/finish/pallas_call | solution.py:455

commit v5 on v4

--- a/solution.py
+++ b/solution.py
@@ -202,11 +202,6 @@
             new = vs[k - 1]
             lean_rows[k - 1, 0] = (new - row_sum(point[...] * new) * point[...]).astype(BF16)
 
-        @pl.when(k == 1)
-        def _():
-            square = vs[0] * vs[0]
-            ar_own[0, 0] = lane_sums([lam[...] * square, square])
-            reduce_send(0, 0)
 
         @pl.when(k == 0)
         def _():
@@ -242,8 +237,9 @@
 
         @pl.when(k == 1)
         def _():
-            ar_own[0, 1] = reduce_take(0, 0)
-            reduce_send(0, 1)
+            square = vs[0] * vs[0]
+            ar_own[0, 0] = lane_sums([lam[...] * square, square])
+            reduce_send(0, 0)
 
         @pl.when(k == 0)
         def _():
@@ -282,6 +278,11 @@
             r = (y + dy) % NY
             halves[p, 0, r] = acc_far[pl.ds(pl.multiple_of(r * SIDE, SIDE), SIDE), :].astype(BF16)
             core_copy(dy).start()
+        @pl.when(k == 1)
+        def _():
+            ar_own[0, 1] = reduce_take(0, 0)
+            reduce_send(0, 1)
+
         multiply(acc, 0, *RUNS[-1])
 
         @pl.when(k == ITERS)

time: 96.4 us -> 96.1 us (level)
  no operation moved by 1% of the time
where the time goes in v5:
time: 96.1 us; the launch traced here: 96 us
  Pallas kernels  94.7 us (99%)
  between operations  1.28 us (1%)
    pallas_call x1, Pallas kernels, shards(): pl.pallas_call(functools.partial(kernel, slots), out_shape=[jax.ShapeDtyp...  93.2 us

profile of v5, /device:TPU:1, one launch (start us, length us, event | category | flops | bytes accessed | tf_op | source)
XLA Modules:
  0.0 96.0 jit_solution(8056533560907593559)
XLA Ops:
  1.3 93.2 %trust_step.1 = (f32[128,128]{1,0:T(8,128)}, f32[128,128]{1,0:T(8,128)}) custom-call(f32[128,128]{1,0:T(8,128)} %y_hbm.1, f32[128,128]{1,0:T(8,128)} %step_hbm.1, s32[1,1]{1,0:T(1,128)} %bitcast.4.accept_hbm, s32[1,192]{1,0:T(1,128)} %bitcast.6, s32[1,192]{1,0:T(1,128)} %bitcast.7, bf16[192,128,128]{2,1,0:T(8,128)(2,1)} %bitcast.5), custom_call_target="tpu_custom_call" | custom-call | flops 4300000256 | bytes 7000000 | tf_op jit(solution)/shard_map/trust_step/pallas_call | solution.py:403
  94.5 1.5 %finish.1 = (f32[128,128]{1,0:T(8,128)}, f32[128,128]{1,0:T(8,128)}) custom-call(f32[128,128]{1,0:T(8,128)} %get-tuple-element.4.step_ref, f32[128,128]{1,0:T(8,128)} %get-tuple-element.5.res_ref), custom_call_target="tpu_custom_call" | custom-call | tf_op jit(solution)/shard_map/finish/pallas_call | solution.py:456
